TPU v7x, 32 devices: a whole 2x2x4 slice. The times are simulated.
32 devices in a mesh: ctx: 8 (over z, y), head: 4 (over x, core).
Axes of the slice: x: 2, y: 2, z: 4, core: 2. Of those that a mesh axis runs over, the one named last changes fastest.
Arguments:
- queries: bfloat16 [2048, 2048], P('ctx', 'head'), may hold values from -34 to 34
- keys: bfloat16 [2048, 2048], P('ctx', 'head'), may hold values from -34 to 34
- values: bfloat16 [2048, 2048], P('ctx', 'head'), may hold values from -6 to 6
- output_grad: bfloat16 [2048, 4096], P('ctx', 'head'), may hold values from -6 to 6
- out_weight: bfloat16 [2048, 4096], P('head'), may hold values from -0.125 to 0.125
- random_blocks: int32 [16, 32, 3], replicated, may hold values from 0 to 31, as said below
- global_blocks: int32 [2], replicated, may hold values from 0 to 31, as said below
Outputs:
- output: bfloat16 [2048, 4096], P('ctx', 'head')
- query_grad: bfloat16 [2048, 2048], P('ctx', 'head')
- key_grad: bfloat16 [2048, 2048], P('ctx', 'head')
- value_grad: bfloat16 [2048, 2048], P('ctx', 'head')
Inputs may be any that keep to these rules, and one draw needn't show every extreme that they name: Every entry random_blocks[h, i, r] names a block j with j // 4 != i // 4. For each group of 4 heads (heads g * 4 to (g + 1) * 4 - 1) and each aligned run of 4 query blocks, the 48 entries name blocks of any one other run at most 7 times, and of some run exactly 7 times. `global_blocks`: the 2 entries are distinct, and one of them is the last block.
All inputs are finite; a program needn't handle non-finite values.
Results may differ from a plain program's by a relative error of at most 0.027.
Values may be sent and summed in bfloat16 or wider, within the bound.
A program may use at most 128 MiB of HBM per device.

v0:
```python
import jax
import jax.numpy as jnp
from jax import lax
from jax.sharding import PartitionSpec as P

HD = 128
BLK = 64
R = 3
G = 2


def with_halo(cells, sides, width):
    for axis, dim in sides:
        count = lax.axis_size(axis)
        ends = count - 1
        head = lax.slice_in_dim(cells, 0, width, axis=dim)
        tail = lax.slice_in_dim(cells, cells.shape[dim] - width, cells.shape[dim], axis=dim)
        cells = jnp.concatenate(
            [
                lax.ppermute(tail, axis, [(i, (i + 1) % count) for i in range(ends)]),
                cells,
                lax.ppermute(head, axis, [((i + 1) % count, i) for i in range(ends)]),
            ],
            axis=dim,
        )
    return cells


def send_plan(request_table, shards, blocks, my_shard):
    requests = request_table.shape[1]
    owners = request_table // blocks
    within = request_table % blocks
    request_ids = jnp.arange(requests, dtype=jnp.int32)
    earlier = (owners[:, :, None] == owners[:, None, :]) & (
        request_ids[None, None, :] < request_ids[None, :, None]
    )
    ranking = jnp.sum(earlier.astype(jnp.int32), axis=2)
    capacity = (requests + shards - 2) // (shards - 1)
    slot_ids = jnp.arange(capacity, dtype=jnp.int32)
    owned = (owners == my_shard)[:, None, :] & (ranking[:, None, :] == slot_ids[None, :, None])
    tile_ids = (request_ids // (blocks * R))[None, :] * blocks + within
    send_tiles = jnp.sum(jnp.where(owned, tile_ids[:, None, :], 0), axis=2).reshape(-1)
    send_alive = jnp.any(owned, axis=2).reshape(-1)
    my_owners = lax.dynamic_index_in_dim(owners, my_shard, 0, keepdims=False)
    my_ranks = lax.dynamic_index_in_dim(ranking, my_shard, 0, keepdims=False)
    return (send_tiles, send_alive, my_owners * capacity + my_ranks)


def pick_tiles(pair_tiles, send_tiles, blocks):
    return pair_tiles[send_tiles % blocks, :, send_tiles // blocks, :]


def pair_products(row_tiles, window, global_pairs, fetched, low_edge, high_edge):
    nearby = jnp.einsum(
        "nqhd,nwbhd->nhqwb",
        row_tiles,
        window[..., low_edge:high_edge],
        preferred_element_type=jnp.float32,
    )
    distant = jnp.einsum(
        "nqhd,gbhd->nhqgb",
        row_tiles,
        global_pairs[..., low_edge:high_edge],
        preferred_element_type=jnp.float32,
    )
    chance = jnp.einsum(
        "nqhd,hnrbd->nhqrb",
        row_tiles,
        fetched[..., low_edge:high_edge],
        preferred_element_type=jnp.float32,
    )
    return jnp.concatenate([nearby, distant, chance], axis=3)


def collect_rows(mixing, window, global_pairs, fetched, low_edge, high_edge):
    nearby = jnp.einsum(
        "nhqwb,nwbhd->nqhd",
        mixing[:, :, :, :3],
        window[..., low_edge:high_edge],
        preferred_element_type=jnp.float32,
    )
    distant = jnp.einsum(
        "nhqgb,gbhd->nqhd",
        mixing[:, :, :, 3 : 3 + G],
        global_pairs[..., low_edge:high_edge],
        preferred_element_type=jnp.float32,
    )
    chance = jnp.einsum(
        "nhqrb,hnrbd->nqhd",
        mixing[:, :, :, 3 + G :],
        fetched[..., low_edge:high_edge],
        preferred_element_type=jnp.float32,
    )
    return nearby + distant + chance


def tile_terms(mixing, row_tiles):
    nearby = jnp.einsum(
        "nhqwb,nqhd->nwbhd", mixing[:, :, :, :3], row_tiles, preferred_element_type=jnp.float32
    )
    distant = jnp.einsum(
        "nhqgb,nqhd->gbhd",
        mixing[:, :, :, 3 : 3 + G],
        row_tiles,
        preferred_element_type=jnp.float32,
    )
    chance = jnp.einsum(
        "nhqrb,nqhd->hnrbd", mixing[:, :, :, 3 + G :], row_tiles, preferred_element_type=jnp.float32
    )
    return (nearby, distant, chance)


def body(queries, keys, values, output_grad, out_weight, random_blocks, global_blocks):
    shards = lax.axis_size("ctx")
    my_shard = lax.axis_index("ctx")
    head_group = lax.axis_index("head")
    tok_local, width_local = queries.shape
    head_dim = HD
    heads_local = width_local // head_dim
    blocks = tok_local // BLK
    scaling = head_dim ** (-0.5)
    query_tiles = queries.reshape(blocks, BLK, heads_local, head_dim)
    pair_tiles = jnp.concatenate(
        [
            keys.reshape(blocks, BLK, heads_local, head_dim),
            values.reshape(blocks, BLK, heads_local, head_dim),
        ],
        axis=3,
    )
    head_table = lax.dynamic_slice_in_dim(random_blocks, head_group * heads_local, heads_local, 0)
    request_table = (
        head_table.reshape(heads_local, shards, blocks, R)
        .transpose(1, 0, 2, 3)
        .reshape(shards, heads_local * blocks * R)
    )
    send_tiles, send_alive, receive_rows = send_plan(request_table, shards, blocks, my_shard)
    received = lax.all_to_all(
        pick_tiles(pair_tiles, send_tiles, blocks), "ctx", split_axis=0, concat_axis=0, tiled=True
    )
    fetched = received[receive_rows].reshape(heads_local, blocks, R, BLK, 2 * head_dim)
    padded = with_halo(pair_tiles.reshape(tok_local, 2 * width_local), (("ctx", 0),), BLK)
    padded = padded.reshape(blocks + 2, BLK, heads_local, 2 * head_dim)
    window = jnp.stack([padded[offset : offset + blocks] for offset in range(3)], axis=1)
    global_owner = global_blocks // blocks
    global_local = global_blocks % blocks
    picked = pair_tiles[global_local]
    holding = jnp.where(
        (global_owner == my_shard)[:, None, None, None], picked.astype(jnp.float32), 0.0
    )
    global_pairs = lax.psum(holding, "ctx").astype(jnp.bfloat16)
    first_block = my_shard * blocks
    window_ids = first_block + jnp.arange(blocks)[:, None] + jnp.arange(3)[None, :] - 1
    inside = (window_ids >= 0) & (window_ids < blocks * shards)
    alive_mask = jnp.concatenate([inside, jnp.ones((blocks, G + R), dtype=bool)], axis=1)[
        :, None, None, :, None
    ]
    logits = jnp.where(
        alive_mask,
        pair_products(query_tiles, window, global_pairs, fetched, 0, head_dim) * scaling,
        -jnp.inf,
    )
    row_max = jnp.max(logits, axis=(3, 4))
    log_total = row_max + jnp.log(jnp.sum(jnp.exp(logits - row_max[..., None, None]), axis=(3, 4)))
    weights_full = jnp.exp(logits - log_total[..., None, None])
    weights_low = weights_full.astype(jnp.bfloat16)
    attended = collect_rows(
        weights_low, window, global_pairs, fetched, head_dim, 2 * head_dim
    ).astype(jnp.bfloat16)
    attended_flat = attended.reshape(tok_local, width_local)
    partial_value = jnp.dot(attended_flat, out_weight, preferred_element_type=jnp.float32)
    output = lax.psum_scatter(partial_value, "head", scatter_dimension=1, tiled=True).astype(
        jnp.bfloat16
    )
    grad_sum = lax.dot_general(
        lax.all_gather(output_grad, "head", axis=1, tiled=True),
        out_weight,
        (((1,), (1,)), ((), ())),
        preferred_element_type=jnp.float32,
    )
    grad_tiles = grad_sum.astype(jnp.bfloat16).reshape(blocks, BLK, heads_local, head_dim)
    delta_rows = jnp.sum(
        grad_tiles.astype(jnp.float32) * attended.astype(jnp.float32), axis=3
    ).transpose(0, 2, 1)
    products = pair_products(grad_tiles, window, global_pairs, fetched, head_dim, 2 * head_dim)
    logit_grad = (weights_full * (products - delta_rows[..., None, None])).astype(jnp.bfloat16)
    query_grad = (
        (collect_rows(logit_grad, window, global_pairs, fetched, 0, head_dim) * scaling)
        .astype(jnp.bfloat16)
        .reshape(tok_local, width_local)
    )
    key_nearby, key_distant, key_chance = tile_terms(logit_grad, query_tiles)
    value_nearby, value_distant, value_chance = tile_terms(weights_low, grad_tiles)
    nearby_terms = jnp.concatenate([key_nearby * scaling, value_nearby], axis=4)
    framed = sum(
        (
            jnp.pad(nearby_terms[:, offset], ((offset, 2 - offset), (0, 0), (0, 0), (0, 0)))
            for offset in range(3)
        )
    )
    edge_rows = jnp.concatenate([framed[0], framed[blocks + 1]], axis=0).reshape(
        2 * BLK, 2 * width_local
    )
    arrived = with_halo(edge_rows.astype(jnp.bfloat16), (("ctx", 0),), BLK).astype(edge_rows.dtype)
    local_grad = framed[1 : blocks + 1]
    local_grad = local_grad.at[0].add(arrived[:BLK].reshape(BLK, heads_local, 2 * head_dim))
    local_grad = local_grad.at[blocks - 1].add(
        arrived[3 * BLK :].reshape(BLK, heads_local, 2 * head_dim)
    )
    distant_terms = jnp.concatenate([key_distant * scaling, value_distant], axis=3)
    summed = lax.psum(distant_terms, "ctx")
    selector = (
        (global_owner == my_shard)[:, None] & (global_local[:, None] == jnp.arange(blocks)[None, :])
    ).astype(jnp.float32)
    local_grad = local_grad + jnp.einsum(
        "gn,gbhd->nbhd", selector, summed, precision=lax.Precision.HIGHEST
    )
    chance_terms = (
        jnp.concatenate([key_chance * scaling, value_chance], axis=4)
        .astype(jnp.bfloat16)
        .reshape(-1, BLK, 2 * head_dim)
    )
    outgoing_grads = (
        jnp.zeros((send_tiles.shape[0], BLK, 2 * head_dim), jnp.bfloat16)
        .at[receive_rows]
        .set(chance_terms)
    )
    returned = lax.all_to_all(outgoing_grads, "ctx", split_axis=0, concat_axis=0, tiled=True)
    segment_ids = jnp.where(send_alive, send_tiles, heads_local * blocks)
    gathered = jax.ops.segment_sum(
        returned.astype(jnp.float32), segment_ids, num_segments=heads_local * blocks + 1
    )[: heads_local * blocks]
    local_grad = local_grad + gathered.reshape(heads_local, blocks, BLK, 2 * head_dim).transpose(
        1, 2, 0, 3
    )
    key_grad = local_grad[..., :head_dim].astype(jnp.bfloat16).reshape(tok_local, width_local)
    value_grad = local_grad[..., head_dim:].astype(jnp.bfloat16).reshape(tok_local, width_local)
    return (output, query_grad, key_grad, value_grad)


def solution(mesh):
    placed = (
        P("ctx", "head"),
        P("ctx", "head"),
        P("ctx", "head"),
        P("ctx", "head"),
        P("head", None),
        P(),
        P(),
    )
    return jax.shard_map(
        body,
        mesh=mesh,
        in_specs=placed,
        out_specs=(P("ctx", "head"), P("ctx", "head"), P("ctx", "head"), P("ctx", "head")),
        check_vma=False,
    )
```

profile of v0, /device:TPU:0, one launch (start us, length us, event | category | flops | bytes accessed | tf_op | source)
XLA Modules:
  0.0 266.9 jit_solution(3460373470147299995)
XLA Ops:
  11.7 2.1 gather_fusion.1
  13.8 7.4 %all-to-all-start = ((bf16[56,64,256]{2,1,0:T(8,128)(2,1)}), bf16[56,64,256]{2,1,0:T(8,128)(2,1)}, u32[]{:S(2)}, u32[]{:S(2)}) async-start(bf16[56,64,256]{2,1,0:T(8,128)(2,1)} %gather_fusion.1), calls=%async_computation | async-start | bytes 3670016 | tf_op jit(solution)/shard_map/all_to_all | solution.py:137
  21.5 3.9 %collective-permute-start = (bf16[64,1024]{1,0:T(8,128)(2,1)S(1)}, bf16[64,1024]{1,0:T(8,128)(2,1)S(1)}, u32[]{:S(2)}, u32[]{:S(2)}) collective-permute-start(bf16[64,1024]{1,0:T(8,128)(2,1)S(1)} %bitcast.209), channel_id=1, source_target_pairs={{0,4},{4,8},{8,12},{12,16},{16,20},{20,24},{24,28},{1,5},{5,9},{9,... | collective-permute-start | bytes 393224 | tf_op jit(solution)/shard_map/ppermute | solution.py:20
  27.7 69.8 %all-reduce.8 = bf16[2,64,4,256]{3,1,2,0:T(8,128)(2,1)S(1)} all-reduce(f32[2,64,4,256]{3,1,2,0:T(8,128)S(1)} %convert_select_fusion), channel_id=1, replica_groups=mesh['ctx'=8,'head'=4] {'ctx'}, use_global_device_ids=true, to_apply=%region_0.1 | all-reduce | flops 131072 | bytes 786432 | tf_op jit(solution)/shard_map/psum | solution.py:150
  104.3 4.1 %convolution_convert_fusion.1 = bf16[256,512]{1,0:T(8,128)(2,1)S(1)} fusion(bf16[256,4096]{1,0:T(8,128)(2,1)} %all-gather.2.cloned.1.call-done, bf16[512,4096]{1,0:T(8,128)(2,1)} %param.15), kind=kOutput, calls=%fused_computation.40 | convolution fusion | flops 1073872896 | bytes 6553600 | tf_op jit(solution)/shard_map/dot_general | solution.py:174
  109.9 2.7 fusion.22
  112.5 3.4 %gather_fusion.2 = bf16[48,64,256]{2,1,0:T(8,128)(2,1)} fusion(bf16[56,64,256]{2,1,0:T(8,128)(2,1)} %all-to-all-done, s32[1024]{0:T(1024)S(1)} %pad_clamp_fusion), kind=kCustom, calls=%fused_computation.2 | custom fusion | bytes 3145920 | tf_op jit(solution)/shard_map/gather | solution.py:140
  115.9 1.6 fusion.96
  125.3 1.5 fusion.2
  129.9 5.4 %fusion.34 = f32[256,4096]{1,0:T(8,128)} fusion(bf16[512,4096]{1,0:T(8,128)(2,1)} %param.15, bf16[32,8,4,128]{3,2,1,0:T(4,128)(2,1)S(1)} %bitcast.194), kind=kOutput, calls=%fused_computation.76 | convolution fusion | flops 1073741824 | bytes 8650752 | tf_op jit(solution)/shard_map/dot_general | solution.py:170
  135.4 1.6 copy-done.3
  140.4 1.5 broadcast_in_dim.82
  141.8 7.6 %scatter_fusion = bf16[56,64,256]{2,1,0:T(8,128)(2,1)} fusion(bf16[56,64,256]{2,1,0:T(8,128)(2,1)} %broadcast_in_dim.82, s32[48]{0:T(128)S(1)} %fusion.85, bf16[48,64,256]{2,1,0:T(8,128)(2,1)} %pad_maximum_fusion.1), kind=kCustom, calls=%fused_computation.3 | custom fusion | bytes 4718784 | tf_op jit(solution)/shard_map/scatter | solution.py:225
  149.5 4.5 %all-to-all-start.1 = ((bf16[56,64,256]{2,1,0:T(8,128)(2,1)}), bf16[56,64,256]{2,1,0:T(8,128)(2,1)}, u32[]{:S(2)}, u32[]{:S(2)}) async-start(bf16[56,64,256]{2,1,0:T(8,128)(2,1)} %scatter_fusion), calls=%async_computation.2 | async-start | bytes 3670016 | tf_op jit(solution)/shard_map/all_to_all | solution.py:227
  155.5 4.1 %collective-permute-start.2 = (bf16[64,1024]{1,0:T(8,128)(2,1)S(1)}, bf16[64,1024]{1,0:T(8,128)(2,1)S(1)}, u32[]{:S(2)}, u32[]{:S(2)}) collective-permute-start(bf16[64,1024]{1,0:T(8,128)(2,1)S(1)} %bitcast.203), channel_id=1, source_target_pairs={{0,4},{4,8},{8,12},{12,16},{16,20},{20,24},{24,28},{1,5},{5,9},{9,... | collective-permute-start | bytes 393224 | tf_op jit(solution)/shard_map/ppermute | solution.py:20
  159.7 1.4 collective-permute-start.3
  163.4 6.2 %collective-permute-done.2 = bf16[64,1024]{1,0:T(8,128)(2,1)S(1)} collective-permute-done((bf16[64,1024]{1,0:T(8,128)(2,1)S(1)}, bf16[64,1024]{1,0:T(8,128)(2,1)S(1)}, u32[]{:S(2)}, u32[]{:S(2)}) %collective-permute-start.2) | collective-permute-done | bytes 131104 | tf_op jit(solution)/shard_map/ppermute | solution.py:20
  169.7 2.6 collective-permute-done.3
  173.7 38.0 %all-reduce.7.cloned.1.call-done = f32[2,64,4,256]{3,1,2,0:T(8,128)} async-done(((f32[2,64,4,256]{3,1,2,0:T(8,128)}), f32[2,64,4,256]{3,1,2,0:T(8,128)}) %all-reduce.7.cloned.1.call-update) | async-done | bytes 524304 | tf_op jit(solution)/shard_map/psum | solution.py:210
  211.7 2.6 fusion.32
  214.3 3.8 %convert_element_type.63 = f32[56,64,256]{2,1,0:T(8,128)} convert(bf16[56,64,256]{2,1,0:T(8,128)(2,1)} %all-to-all-done.1) | non-fusion elementwise | flops 917504 | bytes 5505024 | tf_op jit(solution)/shard_map/convert_element_type | solution.py:230
  218.2 9.1 %scatter_fusion.1 = f32[17,64,256]{2,1,0:T(8,128)S(1)} fusion(f32[17,64,256]{2,1,0:T(8,128)S(1)} %broadcast_in_dim.80, s32[56]{0:T(128)S(1)} %get-tuple-element.53, f32[56,64,256]{2,1,0:T(8,128)} %convert_element_type.63), kind=kCustom, calls=%fused_computation.4 | custom fusion | flops 917504 | bytes 11010272 | tf_op jit(solution)/shard_map/scatter-add | solution.py:229
  229.6 28.7 %reduce-scatter.2.cloned.1.call-done = f32[256,1024]{1,0:T(8,128)} async-done(((f32[256,4096]{1,0:T(8,128)}), f32[256,1024]{1,0:T(8,128)}) %reduce-scatter.2.cloned.1.call-update) | async-done | bytes 1048592 | tf_op jit(solution)/shard_map/reduce_scatter | solution.py:171
  258.3 2.1 convert_element_type.56
  (156 shorter events, 36.7 us)
Async XLA Ops:
  7.2 97.1 %all-gather.2.cloned.1.call-start = ((), (), s32[]{:S(2)}) async-start(), calls=%async_computation.4 | async-start | bytes 2621440 | tf_op jit(solution)/shard_map/all_gather | solution.py:175
  13.8 13.0 %copy-start.24 = (s32[2]{0:T(128)S(1)}, s32[2]{0:T(128)}, u32[]{:S(2)}) copy-start(s32[2]{0:T(128)} %param.17) | copy-start | bytes 28
  13.8 13.0 %copy-start.21 = (bf16[256,512]{1,0:T(8,128)(2,1)S(1)}, bf16[256,512]{1,0:T(8,128)(2,1)}, u32[]{:S(2)}) copy-start(bf16[256,512]{1,0:T(8,128)(2,1)} %param.11) | copy-start | bytes 786436
  13.8 98.7 %all-to-all-start = ((bf16[56,64,256]{2,1,0:T(8,128)(2,1)}), bf16[56,64,256]{2,1,0:T(8,128)(2,1)}, u32[]{:S(2)}, u32[]{:S(2)}) async-start(bf16[56,64,256]{2,1,0:T(8,128)(2,1)} %gather_fusion.1), calls=%async_computation | async-start | bytes 3670016 | tf_op jit(solution)/shard_map/all_to_all | solution.py:137
  21.2 190.5 %all-reduce.7.cloned.1.call-start = ((), (), s32[]{:S(2)}) async-start(), calls=%async_computation.5 | async-start | bytes 1048576 | tf_op jit(solution)/shard_map/psum | solution.py:210
  21.5 77.7 %collective-permute-start = (bf16[64,1024]{1,0:T(8,128)(2,1)S(1)}, bf16[64,1024]{1,0:T(8,128)(2,1)S(1)}, u32[]{:S(2)}, u32[]{:S(2)}) collective-permute-start(bf16[64,1024]{1,0:T(8,128)(2,1)S(1)} %bitcast.209), channel_id=1, source_target_pairs={{0,4},{4,8},{8,12},{12,16},{16,20},{20,24},{24,28},{1,5},{5,9},{9,... | collective-permute-start | bytes 393224 | tf_op jit(solution)/shard_map/ppermute | solution.py:20
  25.5 73.7 %collective-permute-start.1 = (bf16[64,1024]{1,0:T(8,128)(2,1)S(1)}, bf16[64,1024]{1,0:T(8,128)(2,1)S(1)}, u32[]{:S(2)}, u32[]{:S(2)}) collective-permute-start(bf16[64,1024]{1,0:T(8,128)(2,1)S(1)} %bitcast.210), channel_id=1, source_target_pairs={{4,0},{8,4},{12,8},{16,12},{20,16},{24,20},{28,24},{5,1},{9,5},{13... | collective-permute-start | bytes 393224 | tf_op jit(solution)/shard_map/ppermute | solution.py:22
  26.9 75.8 %copy-start.9 = (bf16[4,64,4,128]{3,2,1,0:T(4,128)(2,1)}, bf16[4,64,4,128]{3,2,1,0:T(4,128)(2,1)S(1)}, u32[]{:S(2)}) copy-start(bf16[4,64,4,128]{3,2,1,0:T(4,128)(2,1)S(1)} %reshape.468) | copy-start | bytes 786436
  104.2 4.3 %copy-start.17 = (bf16[2,64,4,128]{3,1,2,0:T(8,128)(2,1)S(1)}, bf16[2,64,4,128]{3,1,2,0:T(8,128)(2,1)}, u32[]{:S(2)}) copy-start(bf16[2,64,4,128]{3,1,2,0:T(8,128)(2,1)} %get-tuple-element.51) | copy-start | bytes 393220
  115.9 2.5 copy-start.10
  122.3 1.5 copy-start.4
  123.5 1.8 copy-start.16
  129.4 128.8 %reduce-scatter.2.cloned.1.call-start = ((), (), s32[]{:S(2)}) async-start(), calls=%async_computation.3 | async-start | bytes 5242880 | tf_op jit(solution)/shard_map/reduce_scatter | solution.py:171
  135.3 1.6 copy-start.3
  135.3 1.6 copy-start.11
  136.9 1.6 copy-start.5
  149.5 64.9 %all-to-all-start.1 = ((bf16[56,64,256]{2,1,0:T(8,128)(2,1)}), bf16[56,64,256]{2,1,0:T(8,128)(2,1)}, u32[]{:S(2)}, u32[]{:S(2)}) async-start(bf16[56,64,256]{2,1,0:T(8,128)(2,1)} %scatter_fusion), calls=%async_computation.2 | async-start | bytes 3670016 | tf_op jit(solution)/shard_map/all_to_all | solution.py:227
  155.0 6.2 %copy-start.8 = (bf16[4,3,64,4,256]{4,2,1,3,0:T(8,128)(2,1)S(1)}, bf16[4,3,64,4,256]{4,2,1,3,0:T(8,128)(2,1)}, u32[]{:S(2)}) copy-start(bf16[4,3,64,4,256]{4,2,1,3,0:T(8,128)(2,1)} %copy-done.6) | copy-start | bytes 4718596
  155.3 7.1 %copy-start.15 = (f32[6,64,4,256]{3,1,2,0:T(8,128)}, f32[6,64,4,256]{3,1,2,0:T(8,128)S(1)}, u32[]{:S(2)}) copy-start(f32[6,64,4,256]{3,1,2,0:T(8,128)S(1)} %get-tuple-element.29) | copy-start | bytes 4718596
  155.3 6.3 %copy-start.13 = (bf16[4,4,3,64,128]{4,3,2,1,0:T(8,128)(2,1)S(1)}, bf16[4,4,3,64,128]{4,3,2,1,0:T(8,128)(2,1)}, u32[]{:S(2)}) copy-start(bf16[4,4,3,64,128]{4,3,2,1,0:T(8,128)(2,1)} %copy-done.12) | copy-start | bytes 2359300
  155.5 14.2 %collective-permute-start.2 = (bf16[64,1024]{1,0:T(8,128)(2,1)S(1)}, bf16[64,1024]{1,0:T(8,128)(2,1)S(1)}, u32[]{:S(2)}, u32[]{:S(2)}) collective-permute-start(bf16[64,1024]{1,0:T(8,128)(2,1)S(1)} %bitcast.203), channel_id=1, source_target_pairs={{0,4},{4,8},{8,12},{12,16},{16,20},{20,24},{24,28},{1,5},{5,9},{9,... | collective-permute-start | bytes 393224 | tf_op jit(solution)/shard_map/ppermute | solution.py:20
  159.7 2.3 copy-start.19
  159.7 12.6 %collective-permute-start.3 = (bf16[64,1024]{1,0:T(8,128)(2,1)S(1)}, bf16[64,1024]{1,0:T(8,128)(2,1)S(1)}, u32[]{:S(2)}, u32[]{:S(2)}) collective-permute-start(bf16[64,1024]{1,0:T(8,128)(2,1)S(1)} %bitcast.205), channel_id=1, source_target_pairs={{4,0},{8,4},{12,8},{16,12},{20,16},{24,20},{28,24},{5,1},{9,5},{13... | collective-permute-start | bytes 393224 | tf_op jit(solution)/shard_map/ppermute | solution.py:22
  228.1 32.2 %copy-start.1 = (s32[16,32,3]{1,0,2:T(8,128)S(1)}, s32[16,32,3]{1,0,2:T(8,128)}, u32[]{:S(2)}) copy-start(s32[16,32,3]{1,0,2:T(8,128)} %param.16) | copy-start | bytes 18436
  (10 other events, 10.7 us)
Sparse Core Ops, SparseCore 0:
  9.6 25.2 all-gather.1
  129.6 82.1 all-reduce.6
  214.4 43.7 reduce-scatter.1
where the time goes:
time: 268 us; the launch traced here: 267 us
  waiting for transfers between devices  76.3 us (28%)
  blocking collectives  69.8 us (26%)
  local copies, waits for them, and re-layouts  33.9 us (13%)
  other arithmetic  26.7 us (10%)
  starting transfers between devices  22.9 us (9%)
  matrix products  22.6 us (8%)
  between operations  14.6 us (5%)
    psum x1, blocking collectives, body(): global_pairs = lax.psum(holding, 'ctx').astype(jnp.bfloat16)  69.8 us
    psum x1, waiting for transfers between devices, body(): summed = lax.psum(distant_terms, 'ctx')  38 us
    reduce_scatter x1, waiting for transfers between devices, body(): lax.psum_scatter(partial_value, 'head', scatter_dimension=1, tiled=True)  28.7 us
    unnamed x57, local copies, waits for them, and re-layouts  9.25 us
    scatter-add x1, other arithmetic, body(): jax.ops.segment_sum(returned.astype(jnp.float32), segment_ids, num_segmen...  9.06 us
    ppermute x2, starting transfers between devices, with_halo(): lax.ppermute(tail, axis, [(i, (i + 1) % count) for i in range(ends)])  7.94 us
    scatter x1, local copies, waits for them, and re-layouts, body(): outgoing_grads = jnp.zeros((send_tiles.shape[0], BLK, 2 * head_dim), jnp....  7.62 us
    all_to_all x1, starting transfers between devices, body(): lax.all_to_all(pick_tiles(pair_tiles, send_tiles, blocks), 'ctx', split_a...  7.41 us
  transfers between devices with their start and end apart: 9, of which 4 were waited for; matrix products, arithmetic and copies ran while one was open for 22% of the time, Pallas kernels for 0%

commit v1 on v0

--- a/solution.py
+++ b/solution.py
@@ -1,6 +1,10 @@
+import functools
+
 import jax
 import jax.numpy as jnp
 from jax import lax
+from jax.experimental import pallas as pl
+from jax.experimental.pallas import tpu as pltpu
 from jax.sharding import PartitionSpec as P
 
 HD = 128
@@ -237,7 +241,422 @@
     return (output, query_grad, key_grad, value_grad)
 
 
+MESH = pl.DeviceIdType.MESH
+YN = 2
+ZN = 4
+HN = 4
+PARTS = ((0, 48, True), (48, 160, False), (160, 256, False))
+NP = len(PARTS)
+
+
+def greet(z, y, head):
+    bar = pltpu.get_barrier_semaphore()
+
+    def hello(target):
+        pl.semaphore_signal(bar, inc=1, device_id=target, device_id_type=MESH)
+
+    hello({"ctx": z * YN + (1 - y)})
+    for d in range(1, HN):
+        hello({"head": lax.rem(head + d, HN)})
+
+    @pl.when(z > 0)
+    def _():
+        hello({"ctx": (z - 1) * YN + y})
+
+    @pl.when(z < ZN - 1)
+    def _():
+        hello({"ctx": (z + 1) * YN + y})
+
+    lower = jnp.where(z > 0, 1, 0)
+    upper = jnp.where(z < ZN - 1, 1, 0)
+    pl.semaphore_wait(bar, HN + lower + upper)
+
+
+def gather_kernel(k_ref, v_ref, og_ref, w_hbm, kv_ref, do_ref, ogbuf, wbuf, acc, wsem, ssem, rsem, hs, hr):
+    me = lax.axis_index("ctx")
+    head = lax.axis_index("head")
+    z, y = me // YN, lax.rem(me, YN)
+    width = k_ref.shape[1]
+    cols = og_ref.shape[1]
+    wcopy = pltpu.make_async_copy(w_hbm, wbuf, wsem)
+    wcopy.start()
+    kv_ref[me, :, :width] = k_ref[...]
+    kv_ref[me, :, width:] = v_ref[...]
+    greet(z, y, head)
+
+    def copy(way, slot, p):
+        lo, hi, _ = PARTS[p]
+        at = kv_ref.at[slot, pl.ds(lo, hi - lo)]
+        target = (z + 1) * YN + y if way == 0 else (z - 1) * YN + y if way == 1 else z * YN + (1 - y)
+        return pltpu.make_async_remote_copy(
+            src_ref=at,
+            dst_ref=at,
+            send_sem=ssem.at[(way * 8 + slot) * NP + p],
+            recv_sem=rsem.at[slot * NP + p],
+            device_id={"ctx": target},
+            device_id_type=MESH,
+        )
+
+    def onward(way, slot, p, act):
+        inside = z < ZN - 1 if way == 0 else z > 0
+
+        @pl.when(inside)
+        def _():
+            act(copy(way, slot, p))
+
+    def run(act, waiting):
+        for p in range(NP):
+            act(copy(2, me, p))
+            onward(0, me, p, act)
+            onward(1, me, p, act)
+        if not waiting:
+            send_heads()
+            multiply(0)
+        other = z * YN + (1 - y)
+        for p in range(NP):
+            if PARTS[p][2]:
+                if not waiting:
+                    copy(2, other, p).wait_recv()
+                onward(0, other, p, act)
+                onward(1, other, p, act)
+        for t in range(1, ZN):
+            for p in range(NP):
+                for way in range(2):
+                    zs = z - t if way == 0 else z + t
+
+                    @pl.when((zs >= 0) & (zs < ZN))
+                    def _():
+                        slot = zs * YN + y
+                        if not waiting:
+                            copy(2, slot, p).wait_recv()
+                        onward(way, slot, p, act)
+                        if PARTS[p][2]:
+                            over = zs * YN + (1 - y)
+                            if not waiting:
+                                copy(2, over, p).wait_recv()
+                            onward(way, over, p, act)
+                        else:
+                            act(copy(2, slot, p))
+            if not waiting:
+                multiply(t)
+        if not waiting:
+            for zs in range(ZN):
+                for p in range(NP):
+                    if not PARTS[p][2]:
+                        copy(2, zs * YN + (1 - y), p).wait_recv()
+
+    order = (0, 1, 2, 3)
+
+    def head_copy(d):
+        return pltpu.make_async_remote_copy(
+            src_ref=og_ref,
+            dst_ref=ogbuf.at[d - 1],
+            send_sem=hs.at[d - 1],
+            recv_sem=hr.at[d - 1],
+            device_id={"head": lax.rem(head + d, HN)},
+            device_id_type=MESH,
+        )
+
+    def send_heads():
+        for d in range(1, HN):
+            head_copy(d).start()
+        wcopy.wait()
+
+    def multiply(d):
+        source = lax.rem(head - order[d] + HN, HN)
+        if d:
+            head_copy(d).wait_recv()
+        shard = og_ref[...] if d == 0 else ogbuf[d - 1]
+        weight = wbuf[:, pl.ds(pl.multiple_of(source * cols, cols), cols)]
+        product = lax.dot_general(
+            shard, weight, (((1,), (1,)), ((), ())), preferred_element_type=jnp.float32
+        )
+        if d == 0:
+            acc[...] = product
+        else:
+            acc[...] += product
+
+    run(lambda c: c.start(), False)
+    do_ref[...] = acc[...].astype(jnp.bfloat16)
+    run(lambda c: c.wait_send(), True)
+    for d in range(1, HN):
+        head_copy(d).wait_send()
+
+
+def local_kernel(rb, gb, q_ref, kv_ref, do_ref, w_ref, out_ref, dq_ref, dkv_ref, acc, att_ref):
+    me = lax.axis_index("ctx")
+    group = lax.axis_index("head")
+    nblk = kv_ref.shape[0]
+    blocks = q_ref.shape[0] // BLK
+    width = q_ref.shape[1]
+    heads = width // HD
+    scaling = HD ** (-0.5)
+    acc[...] = jnp.zeros_like(acc)
+    nt = (((1,), (1,)), ((), ()))
+    tn = (((0,), (0,)), ((), ()))
+    nn = (((1,), (0,)), ((), ()))
+
+    def dot(a, b, dims):
+        return lax.dot_general(a, b, dims, preferred_element_type=jnp.float32)
+
+    def step(n, carry):
+        i = me * blocks + n
+        rows = pl.ds(pl.multiple_of(n * BLK, BLK), BLK)
+        column = lax.broadcasted_iota(jnp.int32, (BLK, 8 * BLK), 1)
+        first_end = jnp.where(i == 0, BLK, 0)
+        last_end = jnp.where(i == nblk - 1, 3 * BLK, 2 * BLK)
+        dead = (column < first_end) | ((column >= 2 * BLK) & (column < last_end))
+        for h in range(heads):
+            hc = slice(h * HD, (h + 1) * HD)
+            vc = slice(width + h * HD, width + (h + 1) * HD)
+            base = ((group * heads + h) * nblk + i) * R
+            ids = [jnp.maximum(i - 1, 0), i, jnp.minimum(i + 1, nblk - 1), gb[0], gb[1]]
+            ids = ids + [rb[base + r] for r in range(R)]
+            kg = jnp.concatenate([kv_ref[e, :, hc] for e in ids], axis=0)
+            vg = jnp.concatenate([kv_ref[e, :, vc] for e in ids], axis=0)
+            q = q_ref[rows, hc]
+            do = do_ref[rows, hc]
+            logits = jnp.where(dead, -jnp.inf, dot(q, kg, nt) * scaling)
+            e = jnp.exp(logits - jnp.max(logits, axis=1, keepdims=True))
+            weights = e * (1.0 / jnp.sum(e, axis=1, keepdims=True))
+            low = weights.astype(jnp.bfloat16)
+            att = dot(low, vg, nn).astype(jnp.bfloat16)
+            att_ref[rows, hc] = att
+            delta = jnp.sum(do.astype(jnp.float32) * att.astype(jnp.float32), axis=1, keepdims=True)
+            lg = (weights * (dot(do, vg, nt) - delta)).astype(jnp.bfloat16)
+            dq_ref[rows, hc] = (dot(lg, kg, nn) * scaling).astype(jnp.bfloat16)
+            dk = dot(lg, q, tn) * scaling
+            dv = dot(low, do, tn)
+            for k, e in enumerate(ids):
+                acc[e, :, hc] += dk[k * BLK : (k + 1) * BLK]
+                acc[e, :, vc] += dv[k * BLK : (k + 1) * BLK]
+        return carry
+
+    lax.fori_loop(0, blocks, step, 0)
+    cols = out_ref.shape[2]
+    for j in range(out_ref.shape[0]):
+        out_ref[j] = dot(att_ref[...], w_ref[:, j * cols : (j + 1) * cols], nn).astype(jnp.bfloat16)
+    dkv_ref[...] = acc[...].astype(jnp.bfloat16)
+
+
+def reduce_kernel(part_ref, outp_ref, out_ref, dk_ref, dv_ref, acc, rz, ry, ro, sums, ssem, zsem, ysem, hs, hr):
+    me = lax.axis_index("ctx")
+    head = lax.axis_index("head")
+    z, y = me // YN, lax.rem(me, YN)
+    width = dk_ref.shape[1]
+    greet(z, y, head)
+
+    def head_copy(d):
+        target = lax.rem(head + d, HN)
+        return pltpu.make_async_remote_copy(
+            src_ref=outp_ref.at[target],
+            dst_ref=ro.at[d - 1],
+            send_sem=hs.at[d - 1],
+            recv_sem=hr.at[d - 1],
+            device_id={"head": target},
+            device_id_type=MESH,
+        )
+
+    def span(p):
+        return pl.ds(PARTS[p][0], PARTS[p][1] - PARTS[p][0])
+
+    def zcopy(way, slot, p):
+        return pltpu.make_async_remote_copy(
+            src_ref=acc.at[slot, span(p)],
+            dst_ref=rz.at[way, slot, span(p)],
+            send_sem=ssem.at[slot * NP + p],
+            recv_sem=zsem.at[(way * 8 + slot) * NP + p],
+            device_id={"ctx": (jnp.minimum(z + 1, ZN - 1) if way == 0 else jnp.maximum(z - 1, 0)) * YN + y},
+            device_id_type=MESH,
+        )
+
+    def ycopy(source, zd, p):
+        return pltpu.make_async_remote_copy(
+            src_ref=source.at[zd * YN + (1 - y), span(p)],
+            dst_ref=ry.at[zd, span(p)],
+            send_sem=ssem.at[(zd * YN + (1 - y)) * NP + p],
+            recv_sem=ysem.at[zd * NP + p],
+            device_id={"ctx": z * YN + (1 - y)},
+            device_id_type=MESH,
+        )
+
+    def zadd(way, slot, p, total):
+        zcopy(way, slot, p).wait_recv()
+        return total + rz[way, slot, span(p)].astype(jnp.float32)
+
+    def far(act):
+        for t in range(ZN - 1, -1, -1):
+            for way in range(2):
+                if t == 0 and way:
+                    continue
+                zd = z + t if way == 0 else z - t
+
+                @pl.when((zd >= 0) & (zd < ZN))
+                def _():
+                    act(zd, way, t)
+
+    bulk = [p for p in range(NP) if not PARTS[p][2]]
+    fast = [p for p in range(NP) if PARTS[p][2]]
+
+    def start_y(zd, way, t):
+        for p in bulk:
+            ycopy(part_ref, zd, p).start()
+
+    far(start_y)
+    for d in range(1, HN):
+        head_copy(d).start()
+
+    def pass_z(zd, way, t):
+        if t == 0:
+            return
+        behind = z > 0 if way == 0 else z < ZN - 1
+        for slot, p in [(zd * YN + (1 - y), p) for p in fast] + [(zd * YN + y, p) for p in range(NP)]:
+            total = part_ref[slot, span(p)].astype(jnp.float32)
+            if not PARTS[p][2]:
+                ycopy(part_ref, zd, p).wait_recv()
+                total = total + ry[zd, span(p)].astype(jnp.float32)
+            acc[slot, span(p)] = total.astype(jnp.bfloat16)
+
+            @pl.when(behind)
+            def _():
+                acc[slot, span(p)] = zadd(way, slot, p, acc[slot, span(p)].astype(jnp.float32)).astype(
+                    jnp.bfloat16
+                )
+
+            zcopy(way, slot, p).start()
+
+    far(pass_z)
+
+    def settle(slot, p):
+        sums[span(p)] = part_ref[slot, span(p)].astype(jnp.float32)
+
+        @pl.when(z > 0)
+        def _():
+            sums[span(p)] = zadd(0, slot, p, sums[span(p)])
+
+        @pl.when(z < ZN - 1)
+        def _():
+            sums[span(p)] = zadd(1, slot, p, sums[span(p)])
+
+    other = z * YN + (1 - y)
+    for p in fast:
+        settle(other, p)
+        acc[other, span(p)] = sums[span(p)].astype(jnp.bfloat16)
+        ycopy(acc, z, p).start()
+    total = outp_ref[head].astype(jnp.float32)
+    for d in range(1, HN):
+        head_copy(d).wait_recv()
+        total = total + ro[d - 1].astype(jnp.float32)
+    out_ref[...] = total.astype(jnp.bfloat16)
+    for p in bulk + fast:
+        settle(me, p)
+        ycopy(part_ref if p in bulk else acc, z, p).wait_recv()
+        grad = sums[span(p)] + ry[z, span(p)].astype(jnp.float32)
+        dk_ref[span(p)] = grad[:, :width].astype(jnp.bfloat16)
+        dv_ref[span(p)] = grad[:, width:].astype(jnp.bfloat16)
+
+    def end_y(zd, way, t):
+        for p in bulk:
+            ycopy(part_ref, zd, p).wait_send()
+
+    def end_z(zd, way, t):
+        if t == 0:
+            return
+        for slot, p in [(zd * YN + (1 - y), p) for p in fast] + [(zd * YN + y, p) for p in range(NP)]:
+            zcopy(way, slot, p).wait_send()
+
+    far(end_y)
+    far(end_z)
+    for p in fast:
+        ycopy(acc, z, p).wait_send()
+    for d in range(1, HN):
+        head_copy(d).wait_send()
+
+
+def near_body(queries, keys, values, output_grad, out_weight, random_blocks, global_blocks):
+    rows, width = queries.shape
+    cols = output_grad.shape[1]
+    cn = YN * ZN
+    vmem = pl.BlockSpec(memory_space=pltpu.VMEM)
+    smem = pl.BlockSpec(memory_space=pltpu.SMEM)
+    anywhere = pl.BlockSpec(memory_space=pl.ANY)
+    bf16, f32 = jnp.bfloat16, jnp.float32
+    dma = pltpu.SemaphoreType.DMA
+    kv, grad = pl.pallas_call(
+        gather_kernel,
+        name="gather",
+        out_shape=(
+            jax.ShapeDtypeStruct((cn, rows, 2 * width), bf16),
+            jax.ShapeDtypeStruct((rows, width), bf16),
+        ),
+        in_specs=[vmem, vmem, vmem, anywhere],
+        out_specs=(vmem, vmem),
+        scratch_shapes=[
+            pltpu.VMEM((HN - 1, rows, cols), bf16),
+            pltpu.VMEM(out_weight.shape, bf16),
+            pltpu.VMEM((rows, width), f32),
+            dma,
+            dma((3 * cn * NP,)),
+            dma((cn * NP,)),
+            dma((HN - 1,)),
+            dma((HN - 1,)),
+        ],
+        compiler_params=pltpu.CompilerParams(
+            collective_id=0, has_side_effects=True, vmem_limit_bytes=32 << 20
+        ),
+    )(keys, values, output_grad, out_weight)
+    nblk = cn * rows // BLK
+    outp, dq, part = pl.pallas_call(
+        local_kernel,
+        name="attention",
+        out_shape=(
+            jax.ShapeDtypeStruct((HN, rows, cols), bf16),
+            jax.ShapeDtypeStruct((rows, width), bf16),
+            jax.ShapeDtypeStruct((nblk, BLK, 2 * width), bf16),
+        ),
+        in_specs=[smem, smem, vmem, vmem, vmem, vmem],
+        out_specs=(vmem, vmem, vmem),
+        scratch_shapes=[pltpu.VMEM((nblk, BLK, 2 * width), f32), pltpu.VMEM((rows, width), bf16)],
+        compiler_params=pltpu.CompilerParams(vmem_limit_bytes=48 << 20),
+    )(
+        random_blocks.reshape(-1),
+        global_blocks,
+        queries,
+        kv.reshape(nblk, BLK, 2 * width),
+        grad,
+        out_weight,
+    )
+    out, dk, dv = pl.pallas_call(
+        reduce_kernel,
+        name="reduce",
+        out_shape=(
+            jax.ShapeDtypeStruct((rows, cols), bf16),
+            jax.ShapeDtypeStruct((rows, width), bf16),
+            jax.ShapeDtypeStruct((rows, width), bf16),
+        ),
+        in_specs=[vmem, vmem],
+        out_specs=(vmem, vmem, vmem),
+        scratch_shapes=[
+            pltpu.VMEM((cn, rows, 2 * width), bf16),
+            pltpu.VMEM((2, cn, rows, 2 * width), bf16),
+            pltpu.VMEM((ZN, rows, 2 * width), bf16),
+            pltpu.VMEM((HN - 1, rows, cols), bf16),
+            pltpu.VMEM((rows, 2 * width), f32),
+            dma((cn * NP,)),
+            dma((2 * cn * NP,)),
+            dma((ZN * NP,)),
+            dma((HN - 1,)),
+            dma((HN - 1,)),
+        ],
+        compiler_params=pltpu.CompilerParams(
+            collective_id=1, has_side_effects=True, vmem_limit_bytes=48 << 20
+        ),
+    )(part.reshape(cn, rows, 2 * width), outp)
+    return (out, dq, dk, dv)
+
+
 def solution(mesh):
+    near = mesh.shape["ctx"] == YN * ZN and mesh.shape["head"] == HN
     placed = (
         P("ctx", "head"),
         P("ctx", "head"),
@@ -248,7 +667,7 @@
         P(),
     )
     return jax.shard_map(
-        body,
+        near_body if near else body,
         mesh=mesh,
         in_specs=placed,
         out_specs=(P("ctx", "head"), P("ctx", "head"), P("ctx", "head"), P("ctx", "head")),

time: 268 us -> 133 us (0.50)
  Pallas kernels: 0 us -> 121 us
  waiting for transfers between devices: 76.3 us -> 0 us
  blocking collectives: 69.8 us -> 0 us
  other arithmetic: 26.7 us -> 0 us
  local copies, waits for them, and re-layouts: 33.9 us -> 10.4 us
  starting transfers between devices: 22.9 us -> 0 us
  matrix products: 22.6 us -> 0 us
  between operations: 14.6 us -> 0.69 us
    pallas_call x0 -> x3, Pallas kernels: none -> 121 us  [the longest x1 54.4 us: near_body(): pl.pallas_call(gather_kernel, name='gather', out_shape=(jax.ShapeDtypeStr...]
    psum x1 -> x0, blocking collectives: 69.8 us -> none  [body(): global_pairs = lax.psum(holding, 'ctx').astype(jnp.bfloat16)]
    psum x1 -> x0, waiting for transfers between devices: 38 us -> none  [body(): summed = lax.psum(distant_terms, 'ctx')]
    reduce_scatter x1 -> x0, waiting for transfers between devices: 28.7 us -> none  [body(): lax.psum_scatter(partial_value, 'head', scatter_dimension=1, tiled=True)]
    dot_general x20 -> x0, matrix products: 22.3 us -> none  [the longest x1 5.39 us: body(): jnp.dot(attended_flat, out_weight, preferred_element_type=jnp.float32)]
    all_to_all x2 -> x0, starting transfers between devices: 11.9 us -> none  [the longest x1 7.41 us: body(): lax.all_to_all(pick_tiles(pair_tiles, send_tiles, blocks), 'ctx', split_a...]
    ppermute x4 -> x0, starting transfers between devices: 10.7 us -> none  [the longest x2 7.94 us: with_halo(): lax.ppermute(tail, axis, [(i, (i + 1) % count) for i in range(ends)])]
    scatter-add x3 -> x0, other arithmetic: 10.2 us -> none  [the longest x1 9.06 us: body(): jax.ops.segment_sum(returned.astype(jnp.float32), segment_ids, num_segmen...]
  transfers between devices with their start and end apart: 9 -> 0, of which waited for: 4 -> 0; matrix products, arithmetic and copies ran while one was open for 22% -> 0% of each run, Pallas kernels for 0% -> 0%
where the time goes in v1:
time: 133 us; the launch traced here: 132 us
  Pallas kernels  121 us (91%)
  local copies, waits for them, and re-layouts  10.4 us (8%)
    pallas_call x1, Pallas kernels, near_body(): pl.pallas_call(gather_kernel, name='gather', out_shape=(jax.ShapeDtypeStr...  54.4 us
    pallas_call x1, Pallas kernels, near_body(): pl.pallas_call(reduce_kernel, name='reduce', out_shape=(jax.ShapeDtypeStr...  47.9 us
    pallas_call x1, Pallas kernels, near_body(): pl.pallas_call(local_kernel, name='attention', out_shape=(jax.ShapeDtypeS...  19 us
    unnamed x18, local copies, waits for them, and re-layouts  10.2 us

profile of v1, /device:TPU:0, one launch (start us, length us, event | category | flops | bytes accessed | tf_op | source)
XLA Modules:
  0.0 132.3 jit_solution(10338614733704592345)
XLA Ops:
  0.6 0.0 copy-start.6
  0.6 0.0 copy-start.5
  0.7 1.0 copy.11
  1.6 0.2 reshape.17.rb
  1.8 0.0 copy-start
  1.8 2.2 %copy-done = bf16[512,4096]{1,0:T(8,128)(2,1)S(1)} copy-done((bf16[512,4096]{1,0:T(8,128)(2,1)S(1)}, bf16[512,4096]{1,0:T(8,128)(2,1)}, u32[]{:S(2)}) %copy-start) | copy-done | bytes 4194328
  4.0 0.0 copy-start.2
  4.0 1.0 copy-done.2
  5.0 0.0 copy-start.3
  5.0 0.9 copy-done.3
  6.0 0.0 copy-start.4
  6.0 0.9 copy-done.4
  6.9 54.4 %gather.1 = (bf16[8,256,1024]{2,1,0:T(8,128)(2,1)S(1)}, bf16[256,512]{1,0:T(8,128)(2,1)S(1)}) custom-call(bf16[256,512]{1,0:T(8,128)(2,1)S(1)} %copy-done.3, bf16[256,512]{1,0:T(8,128)(2,1)S(1)} %copy-done.4, bf16[256,1024]{1,0:T(8,128)(2,1)S(1)} %copy-done.2, bf16[512,4096]{1,0:T(8,128)(2,1)S(1)} %copy-done), custom_call_target="tpu_custom_call" | custom-call | tf_op jit(solution)/shard_map/gather/pallas_call | solution.py:585
  61.3 0.0 copy-start.1
  61.3 1.9 %copy-done.1 = bf16[8,256,1024]{2,1,0:T(8,128)(2,1)} copy-done((bf16[8,256,1024]{2,1,0:T(8,128)(2,1)}, bf16[8,256,1024]{2,1,0:T(8,128)(2,1)S(1)}, u32[]{:S(2)}) %copy-start.1) | copy-done | bytes 4194328
  63.3 0.0 copy-done.6
  63.3 0.0 copy-done.5
  63.3 19.0 %attention.1 = (bf16[4,256,1024]{2,1,0:T(8,128)(2,1)S(1)}, bf16[256,512]{1,0:T(8,128)(2,1)}, bf16[32,64,1024]{2,1,0:T(8,128)(2,1)}) custom-call(s32[1536]{0:T(1024)S(1)} %reshape.17.rb, s32[2]{0:T(128)S(1)} %copy-done.6, bf16[256,512]{1,0:T(8,128)(2,1)S(1)} %copy-done.5, bf16[32,64,1024]{2,1,0:T(8,128)(2,1)} %bitcast.2, ...), custom_call_target="tpu_custom_call" | custom-call | tf_op jit(solution)/shard_map/attention/pallas_call | solution.py:609
  82.2 47.9 %reduce.1 = (bf16[256,1024]{1,0:T(8,128)(2,1)S(1)}, bf16[256,512]{1,0:T(8,128)(2,1)S(1)}, bf16[256,512]{1,0:T(8,128)(2,1)S(1)}) custom-call(bf16[8,256,1024]{2,1,0:T(8,128)(2,1)} %bitcast.3, bf16[4,256,1024]{2,1,0:T(8,128)(2,1)S(1)} %get-tuple-element.15.outp_ref), custom_call_target="tpu_custom_call" | custom-call | tf_op jit(solution)/shard_map/reduce/pallas_call | solution.py:629
  130.1 0.8 copy.15
  130.9 0.7 copy.16
  131.6 0.7 copy.17
Async XLA Ops:
  0.6 62.6 %copy-start.6 = (s32[2]{0:T(128)S(1)}, s32[2]{0:T(128)}, u32[]{:S(2)}) copy-start(s32[2]{0:T(128)} %gb.1) | copy-start | bytes 28
  0.6 62.6 %copy-start.5 = (bf16[256,512]{1,0:T(8,128)(2,1)S(1)}, bf16[256,512]{1,0:T(8,128)(2,1)}, u32[]{:S(2)}) copy-start(bf16[256,512]{1,0:T(8,128)(2,1)} %q_ref.1) | copy-start | bytes 786436
  1.8 2.2 %copy-start = (bf16[512,4096]{1,0:T(8,128)(2,1)S(1)}, bf16[512,4096]{1,0:T(8,128)(2,1)}, u32[]{:S(2)}) copy-start(bf16[512,4096]{1,0:T(8,128)(2,1)} %w_ref.1) | copy-start | bytes 12582916
  4.0 1.0 copy-start.2
  5.0 0.9 copy-start.3
  6.0 0.9 copy-start.4
  61.3 1.9 %copy-start.1 = (bf16[8,256,1024]{2,1,0:T(8,128)(2,1)}, bf16[8,256,1024]{2,1,0:T(8,128)(2,1)S(1)}, u32[]{:S(2)}) copy-start(bf16[8,256,1024]{2,1,0:T(8,128)(2,1)S(1)} %get-tuple-element.12) | copy-start | bytes 12582916

commit v2 on v1

--- a/solution.py
+++ b/solution.py
@@ -245,7 +245,7 @@
 YN = 2
 ZN = 4
 HN = 4
-PARTS = ((0, 48, True), (48, 160, False), (160, 256, False))
+PARTS = ((0, 48, True), (48, 128, False), (128, 192, False), (192, 256, False))
 NP = len(PARTS)
 
 
@@ -272,7 +272,7 @@
     pl.semaphore_wait(bar, HN + lower + upper)
 
 
-def gather_kernel(k_ref, v_ref, og_ref, w_hbm, kv_ref, do_ref, ogbuf, wbuf, acc, wsem, ssem, rsem, hs, hr):
+def gather_kernel(k_ref, v_ref, og_ref, w_hbm, kv_ref, do_ref, wbuf, ogbuf, oglocal, acc, wsem, lsem, ssem, rsem, hs, hr):
     me = lax.axis_index("ctx")
     head = lax.axis_index("head")
     z, y = me // YN, lax.rem(me, YN)
@@ -280,9 +280,15 @@
     cols = og_ref.shape[1]
     wcopy = pltpu.make_async_copy(w_hbm, wbuf, wsem)
     wcopy.start()
-    kv_ref[me, :, :width] = k_ref[...]
-    kv_ref[me, :, width:] = v_ref[...]
+    kcopy = pltpu.make_async_copy(k_ref, kv_ref.at[me, :, pl.ds(0, width)], lsem.at[0])
+    vcopy = pltpu.make_async_copy(v_ref, kv_ref.at[me, :, pl.ds(width, width)], lsem.at[1])
+    ogcopy = pltpu.make_async_copy(og_ref, oglocal, lsem.at[2])
+    kcopy.start()
+    vcopy.start()
+    ogcopy.start()
     greet(z, y, head)
+    kcopy.wait()
+    vcopy.wait()
 
     def copy(way, slot, p):
         lo, hi, _ = PARTS[p]
@@ -360,13 +366,14 @@
     def send_heads():
         for d in range(1, HN):
             head_copy(d).start()
+        ogcopy.wait()
         wcopy.wait()
 
     def multiply(d):
         source = lax.rem(head - order[d] + HN, HN)
         if d:
             head_copy(d).wait_recv()
-        shard = og_ref[...] if d == 0 else ogbuf[d - 1]
+        shard = oglocal[...] if d == 0 else ogbuf[d - 1]
         weight = wbuf[:, pl.ds(pl.multiple_of(source * cols, cols), cols)]
         product = lax.dot_general(
             shard, weight, (((1,), (1,)), ((), ())), preferred_element_type=jnp.float32
@@ -383,7 +390,7 @@
         head_copy(d).wait_send()
 
 
-def local_kernel(rb, gb, q_ref, kv_ref, do_ref, w_ref, out_ref, dq_ref, dkv_ref, acc, att_ref):
+def local_kernel(rb, gb, q_ref, kv_ref, do_ref, w_ref, out_ref, dq_ref, dkv_ref, shared, att_ref):
     me = lax.axis_index("ctx")
     group = lax.axis_index("head")
     nblk = kv_ref.shape[0]
@@ -391,7 +398,8 @@
     width = q_ref.shape[1]
     heads = width // HD
     scaling = HD ** (-0.5)
-    acc[...] = jnp.zeros_like(acc)
+    dkv_ref[...] = jnp.zeros_like(dkv_ref)
+    shared[...] = jnp.zeros_like(shared)
     nt = (((1,), (1,)), ((), ()))
     tn = (((0,), (0,)), ((), ()))
     nn = (((1,), (0,)), ((), ()))
@@ -406,12 +414,12 @@
         first_end = jnp.where(i == 0, BLK, 0)
         last_end = jnp.where(i == nblk - 1, 3 * BLK, 2 * BLK)
         dead = (column < first_end) | ((column >= 2 * BLK) & (column < last_end))
+        late = []
         for h in range(heads):
             hc = slice(h * HD, (h + 1) * HD)
             vc = slice(width + h * HD, width + (h + 1) * HD)
-            base = ((group * heads + h) * nblk + i) * R
             ids = [jnp.maximum(i - 1, 0), i, jnp.minimum(i + 1, nblk - 1), gb[0], gb[1]]
-            ids = ids + [rb[base + r] for r in range(R)]
+            ids = ids + [rb[r, group * heads + h, i] for r in range(R)]
             kg = jnp.concatenate([kv_ref[e, :, hc] for e in ids], axis=0)
             vg = jnp.concatenate([kv_ref[e, :, vc] for e in ids], axis=0)
             q = q_ref[rows, hc]
@@ -427,16 +435,25 @@
             dq_ref[rows, hc] = (dot(lg, kg, nn) * scaling).astype(jnp.bfloat16)
             dk = dot(lg, q, tn) * scaling
             dv = dot(low, do, tn)
-            for k, e in enumerate(ids):
-                acc[e, :, hc] += dk[k * BLK : (k + 1) * BLK]
-                acc[e, :, vc] += dv[k * BLK : (k + 1) * BLK]
+            late.append((hc, vc, ids, dk, dv))
+        for hc, vc, ids, dk, dv in late:
+            for g in range(G):
+                shared[g, :, hc] += dk[(3 + g) * BLK : (4 + g) * BLK]
+                shared[g, :, vc] += dv[(3 + g) * BLK : (4 + g) * BLK]
+            for k in (0, 1, 2, 5, 6, 7):
+                for at, term in ((hc, dk), (vc, dv)):
+                    held = dkv_ref[ids[k], :, at].astype(jnp.float32)
+                    held = held + term[k * BLK : (k + 1) * BLK]
+                    dkv_ref[ids[k], :, at] = held.astype(jnp.bfloat16)
         return carry
 
     lax.fori_loop(0, blocks, step, 0)
     cols = out_ref.shape[2]
     for j in range(out_ref.shape[0]):
         out_ref[j] = dot(att_ref[...], w_ref[:, j * cols : (j + 1) * cols], nn).astype(jnp.bfloat16)
-    dkv_ref[...] = acc[...].astype(jnp.bfloat16)
+    for g in range(G):
+        held = dkv_ref[gb[g]].astype(jnp.float32)
+        dkv_ref[gb[g]] = (held + shared[g]).astype(jnp.bfloat16)
 
 
 def reduce_kernel(part_ref, outp_ref, out_ref, dk_ref, dv_ref, acc, rz, ry, ro, sums, ssem, zsem, ysem, hs, hr):
@@ -579,30 +596,32 @@
     cn = YN * ZN
     vmem = pl.BlockSpec(memory_space=pltpu.VMEM)
     smem = pl.BlockSpec(memory_space=pltpu.SMEM)
-    anywhere = pl.BlockSpec(memory_space=pl.ANY)
+    hbm = pl.BlockSpec(memory_space=pltpu.HBM)
     bf16, f32 = jnp.bfloat16, jnp.float32
     dma = pltpu.SemaphoreType.DMA
-    kv, grad = pl.pallas_call(
+    kv, grad, weight = pl.pallas_call(
         gather_kernel,
         name="gather",
         out_shape=(
             jax.ShapeDtypeStruct((cn, rows, 2 * width), bf16),
             jax.ShapeDtypeStruct((rows, width), bf16),
+            jax.ShapeDtypeStruct(out_weight.shape, bf16),
         ),
-        in_specs=[vmem, vmem, vmem, anywhere],
-        out_specs=(vmem, vmem),
+        in_specs=[hbm, hbm, hbm, hbm],
+        out_specs=(vmem, vmem, vmem),
         scratch_shapes=[
             pltpu.VMEM((HN - 1, rows, cols), bf16),
-            pltpu.VMEM(out_weight.shape, bf16),
+            pltpu.VMEM((rows, cols), bf16),
             pltpu.VMEM((rows, width), f32),
             dma,
+            dma((3,)),
             dma((3 * cn * NP,)),
             dma((cn * NP,)),
             dma((HN - 1,)),
             dma((HN - 1,)),
         ],
         compiler_params=pltpu.CompilerParams(
-            collective_id=0, has_side_effects=True, vmem_limit_bytes=32 << 20
+            collective_id=0, has_side_effects=True, vmem_limit_bytes=16 << 20
         ),
     )(keys, values, output_grad, out_weight)
     nblk = cn * rows // BLK
@@ -616,15 +635,15 @@
         ),
         in_specs=[smem, smem, vmem, vmem, vmem, vmem],
         out_specs=(vmem, vmem, vmem),
-        scratch_shapes=[pltpu.VMEM((nblk, BLK, 2 * width), f32), pltpu.VMEM((rows, width), bf16)],
-        compiler_params=pltpu.CompilerParams(vmem_limit_bytes=48 << 20),
+        scratch_shapes=[pltpu.VMEM((G, BLK, 2 * width), f32), pltpu.VMEM((rows, width), bf16)],
+        compiler_params=pltpu.CompilerParams(vmem_limit_bytes=20 << 20),
     )(
-        random_blocks.reshape(-1),
+        random_blocks.transpose(2, 0, 1),
         global_blocks,
         queries,
         kv.reshape(nblk, BLK, 2 * width),
         grad,
-        out_weight,
+        weight,
     )
     out, dk, dv = pl.pallas_call(
         reduce_kernel,
@@ -649,7 +668,7 @@
             dma((HN - 1,)),
         ],
         compiler_params=pltpu.CompilerParams(
-            collective_id=1, has_side_effects=True, vmem_limit_bytes=48 << 20
+            collective_id=1, has_side_effects=True, vmem_limit_bytes=30 << 20
         ),
     )(part.reshape(cn, rows, 2 * width), outp)
     return (out, dq, dk, dv)

time: 133 us -> 120 us (0.902)
  Pallas kernels: 121 us -> 111 us
  local copies, waits for them, and re-layouts: 10.4 us -> 7.34 us
    pallas_call x1, Pallas kernels: 19 us -> 13.8 us  [near_body(): pl.pallas_call(local_kernel, name='attention', out_shape=(jax.ShapeDtypeS...]
    pallas_call x1, Pallas kernels: 47.9 us -> 43.4 us  [near_body(): pl.pallas_call(reduce_kernel, name='reduce', out_shape=(jax.ShapeDtypeStr...]
    unnamed x18 -> x17, local copies, waits for them, and re-layouts: 10.2 us -> 7.34 us
where the time goes in v2:
time: 120 us; the launch traced here: 119 us
  Pallas kernels  111 us (92%)
  local copies, waits for them, and re-layouts  7.34 us (6%)
    pallas_call x1, Pallas kernels, near_body(): pl.pallas_call(gather_kernel, name='gather', out_shape=(jax.ShapeDtypeStr...  54 us
    pallas_call x1, Pallas kernels, near_body(): pl.pallas_call(reduce_kernel, name='reduce', out_shape=(jax.ShapeDtypeStr...  43.4 us
    pallas_call x1, Pallas kernels, near_body(): pl.pallas_call(local_kernel, name='attention', out_shape=(jax.ShapeDtypeS...  13.8 us
    unnamed x17, local copies, waits for them, and re-layouts  7.34 us

profile of v2, /device:TPU:0, one launch (start us, length us, event | category | flops | bytes accessed | tf_op | source)
XLA Modules:
  0.0 119.3 jit_solution(9814982932582999037)
XLA Ops:
  0.6 0.0 copy-start.6
  0.6 0.0 copy-start
  0.7 2.2 %copy-done = bf16[512,4096]{1,0:T(8,128)(2,1)S(1)} copy-done((bf16[512,4096]{1,0:T(8,128)(2,1)S(1)}, bf16[512,4096]{1,0:T(8,128)(2,1)}, u32[]{:S(2)}) %copy-start) | copy-done | bytes 4194328
  2.8 0.0 copy-start.1
  2.8 1.0 copy-done.1
  3.9 0.0 copy-start.2
  3.9 0.9 copy-done.2
  4.8 0.0 copy-start.3
  4.8 0.9 copy-done.3
  5.8 0.0 copy-start.4
  5.8 0.0 copy-start.5
  5.8 54.0 %gather.1 = (bf16[8,256,1024]{2,1,0:T(8,128)(2,1)S(1)}, bf16[256,512]{1,0:T(8,128)(2,1)S(1)}, bf16[512,4096]{1,0:T(8,128)(2,1)S(1)}) custom-call(bf16[256,512]{1,0:T(8,128)(2,1)S(1)} %copy-done.2, bf16[256,512]{1,0:T(8,128)(2,1)S(1)} %copy-done.3, bf16[256,1024]{1,0:T(8,128)(2,1)S(1)} %copy-done.1, bf16[512,4096]{1,0:T(8,128)(2,1)S(1)} %copy-done), custom_call_target="tpu_custom_call" | custom-call | tf_op jit(solution)/shard_map/gather/pallas_call | solution.py:602
  59.8 0.0 copy-done.6
  59.8 0.0 copy-done.4
  59.8 0.0 copy-done.5
  59.9 13.8 %attention.1 = (bf16[4,256,1024]{2,1,0:T(8,128)(2,1)S(1)}, bf16[256,512]{1,0:T(8,128)(2,1)}, bf16[32,64,1024]{2,1,0:T(8,128)(2,1)S(1)}) custom-call(s32[3,16,32]{2,1,0:T(8,128)S(1)} %bitcast.5, s32[2]{0:T(128)S(1)} %copy-done.6, bf16[256,512]{1,0:T(8,128)(2,1)S(1)} %copy-done.4, bf16[32,64,1024]{2,1,0:T(8,128)(2,1)S(1)} %bitcast.4, ...), custom_call_target="tpu_custom_call" | custom-call | tf_op jit(solution)/shard_map/attention/pallas_call | solution.py:628
  73.7 43.4 %reduce.1 = (bf16[256,1024]{1,0:T(8,128)(2,1)S(1)}, bf16[256,512]{1,0:T(8,128)(2,1)S(1)}, bf16[256,512]{1,0:T(8,128)(2,1)S(1)}) custom-call(bf16[8,256,1024]{2,1,0:T(8,128)(2,1)S(1)} %bitcast.3, bf16[4,256,1024]{2,1,0:T(8,128)(2,1)S(1)} %get-tuple-element.17.outp_ref), custom_call_target="tpu_custom_call" | custom-call | tf_op jit(solution)/shard_map/reduce/pallas_call | solution.py:648
  117.1 0.8 copy.14
  117.9 0.7 copy.15
  118.6 0.7 copy.16
Async XLA Ops:
  0.6 59.2 %copy-start.6 = (s32[2]{0:T(128)S(1)}, s32[2]{0:T(128)}, u32[]{:S(2)}) copy-start(s32[2]{0:T(128)} %gb.1) | copy-start | bytes 28
  0.6 2.2 %copy-start = (bf16[512,4096]{1,0:T(8,128)(2,1)S(1)}, bf16[512,4096]{1,0:T(8,128)(2,1)}, u32[]{:S(2)}) copy-start(bf16[512,4096]{1,0:T(8,128)(2,1)} %w_hbm.1) | copy-start | bytes 12582916
  2.8 1.0 copy-start.1
  3.9 0.9 copy-start.2
  4.8 0.9 copy-start.3
  5.8 54.1 %copy-start.4 = (bf16[256,512]{1,0:T(8,128)(2,1)S(1)}, bf16[256,512]{1,0:T(8,128)(2,1)}, u32[]{:S(2)}) copy-start(bf16[256,512]{1,0:T(8,128)(2,1)} %q_ref.1) | copy-start | bytes 786436
  5.8 54.1 %copy-start.5 = (s32[16,32,3]{1,0,2:T(8,128)S(1)}, s32[16,32,3]{1,0,2:T(8,128)}, u32[]{:S(2)}) copy-start(s32[16,32,3]{1,0,2:T(8,128)} %param.12) | copy-start | bytes 18436

commit v3 on v2

--- a/solution.py
+++ b/solution.py
@@ -390,7 +390,7 @@
         head_copy(d).wait_send()
 
 
-def local_kernel(rb, gb, q_ref, kv_ref, do_ref, w_ref, out_ref, dq_ref, dkv_ref, shared, att_ref):
+def local_kernel(rb, gb, q_ref, kv_ref, do_ref, att_ref, dq_ref, dkv_ref, shared):
     me = lax.axis_index("ctx")
     group = lax.axis_index("head")
     nblk = kv_ref.shape[0]
@@ -448,15 +448,12 @@
         return carry
 
     lax.fori_loop(0, blocks, step, 0)
-    cols = out_ref.shape[2]
-    for j in range(out_ref.shape[0]):
-        out_ref[j] = dot(att_ref[...], w_ref[:, j * cols : (j + 1) * cols], nn).astype(jnp.bfloat16)
     for g in range(G):
         held = dkv_ref[gb[g]].astype(jnp.float32)
         dkv_ref[gb[g]] = (held + shared[g]).astype(jnp.bfloat16)
 
 
-def reduce_kernel(part_ref, outp_ref, out_ref, dk_ref, dv_ref, acc, rz, ry, ro, sums, ssem, zsem, ysem, hs, hr):
+def reduce_kernel(part_ref, att_ref, w_ref, out_ref, dk_ref, dv_ref, outp_ref, acc, rz, ry, ro, sums, ssem, zsem, ysem, hs, hr):
     me = lax.axis_index("ctx")
     head = lax.axis_index("head")
     z, y = me // YN, lax.rem(me, YN)
@@ -520,8 +517,16 @@
             ycopy(part_ref, zd, p).start()
 
     far(start_y)
-    for d in range(1, HN):
-        head_copy(d).start()
+    cols = out_ref.shape[1]
+    for d in (2, 1, 3, 0):
+        target = lax.rem(head + d, HN)
+        outp_ref[target] = jnp.dot(
+            att_ref[...],
+            w_ref[:, pl.ds(pl.multiple_of(target * cols, cols), cols)],
+            preferred_element_type=jnp.float32,
+        ).astype(jnp.bfloat16)
+        if d:
+            head_copy(d).start()
 
     def pass_z(zd, way, t):
         if t == 0:
@@ -623,19 +628,19 @@
         compiler_params=pltpu.CompilerParams(
             collective_id=0, has_side_effects=True, vmem_limit_bytes=16 << 20
         ),
-    )(keys, values, output_grad, out_weight)
+    )(*(pltpu.with_memory_space_constraint(x, pltpu.HBM) for x in (keys, values, output_grad, out_weight)))
     nblk = cn * rows // BLK
-    outp, dq, part = pl.pallas_call(
+    att, dq, part = pl.pallas_call(
         local_kernel,
         name="attention",
         out_shape=(
-            jax.ShapeDtypeStruct((HN, rows, cols), bf16),
+            jax.ShapeDtypeStruct((rows, width), bf16),
             jax.ShapeDtypeStruct((rows, width), bf16),
             jax.ShapeDtypeStruct((nblk, BLK, 2 * width), bf16),
         ),
-        in_specs=[smem, smem, vmem, vmem, vmem, vmem],
+        in_specs=[smem, smem, vmem, vmem, vmem],
         out_specs=(vmem, vmem, vmem),
-        scratch_shapes=[pltpu.VMEM((G, BLK, 2 * width), f32), pltpu.VMEM((rows, width), bf16)],
+        scratch_shapes=[pltpu.VMEM((G, BLK, 2 * width), f32)],
         compiler_params=pltpu.CompilerParams(vmem_limit_bytes=20 << 20),
     )(
         random_blocks.transpose(2, 0, 1),
@@ -643,7 +648,6 @@
         queries,
         kv.reshape(nblk, BLK, 2 * width),
         grad,
-        weight,
     )
     out, dk, dv = pl.pallas_call(
         reduce_kernel,
@@ -653,9 +657,10 @@
             jax.ShapeDtypeStruct((rows, width), bf16),
             jax.ShapeDtypeStruct((rows, width), bf16),
         ),
-        in_specs=[vmem, vmem],
+        in_specs=[vmem, vmem, vmem],
         out_specs=(vmem, vmem, vmem),
         scratch_shapes=[
+            pltpu.VMEM((HN, rows, cols), bf16),
             pltpu.VMEM((cn, rows, 2 * width), bf16),
             pltpu.VMEM((2, cn, rows, 2 * width), bf16),
             pltpu.VMEM((ZN, rows, 2 * width), bf16),
@@ -670,7 +675,7 @@
         compiler_params=pltpu.CompilerParams(
             collective_id=1, has_side_effects=True, vmem_limit_bytes=30 << 20
         ),
-    )(part.reshape(cn, rows, 2 * width), outp)
+    )(part.reshape(cn, rows, 2 * width), att, weight)
     return (out, dq, dk, dv)
 
 

time: 120 us -> 118 us (0.983)
  local copies, waits for them, and re-layouts: 7.34 us -> 2.21 us
  Pallas kernels: 111 us -> 115 us
    unnamed x17 -> x9, local copies, waits for them, and re-layouts: 7.34 us -> 2.21 us
    pallas_call x1, Pallas kernels: 43.4 us -> 48.1 us  [near_body(): pl.pallas_call(reduce_kernel, name='reduce', out_shape=(jax.ShapeDtypeStr...]
where the time goes in v3:
time: 118 us
  Pallas kernels  115 us (97%)
  local copies, waits for them, and re-layouts  2.21 us (2%)
    pallas_call x1, Pallas kernels, near_body(): pl.pallas_call(gather_kernel, name='gather', out_shape=(jax.ShapeDtypeStr...  53.8 us
    pallas_call x1, Pallas kernels, near_body(): pl.pallas_call(reduce_kernel, name='reduce', out_shape=(jax.ShapeDtypeStr...  48.1 us
    pallas_call x1, Pallas kernels, near_body(): pl.pallas_call(local_kernel, name='attention', out_shape=(jax.ShapeDtypeS...  13.2 us

profile of v3, /device:TPU:0, one launch (start us, length us, event | category | flops | bytes accessed | tf_op | source)
XLA Modules:
  0.0 118.0 jit_solution(16882321512489541562)
XLA Ops:
  0.6 0.0 copy-start.2
  0.6 0.0 copy-start.1
  0.7 0.0 copy-start
  0.7 53.8 %gather.1 = (bf16[8,256,1024]{2,1,0:T(8,128)(2,1)S(1)}, bf16[256,512]{1,0:T(8,128)(2,1)S(1)}, bf16[512,4096]{1,0:T(8,128)(2,1)S(1)}) custom-call(bf16[256,512]{1,0:T(8,128)(2,1)} %k_ref.1, bf16[256,512]{1,0:T(8,128)(2,1)} %v_ref.1, bf16[256,1024]{1,0:T(8,128)(2,1)} %og_ref.1, bf16[512,4096]{1,0:T(8,128)(2,1)} %w_hbm.1), custom_call_target="tpu_custom_call" | custom-call | tf_op jit(solution)/shard_map/gather/pallas_call | solution.py:607
  54.4 0.0 copy-done.2
  54.4 0.0 copy-done.1
  54.5 0.0 copy-done
  54.5 13.2 %attention.1 = (bf16[256,512]{1,0:T(8,128)(2,1)S(1)}, bf16[256,512]{1,0:T(8,128)(2,1)}, bf16[32,64,1024]{2,1,0:T(8,128)(2,1)S(1)}) custom-call(s32[3,16,32]{2,1,0:T(8,128)S(1)} %bitcast.5, s32[2]{0:T(128)S(1)} %copy-done.2, bf16[256,512]{1,0:T(8,128)(2,1)S(1)} %copy-done, bf16[32,64,1024]{2,1,0:T(8,128)(2,1)S(1)} %bitcast.3, ...), custom_call_target="tpu_custom_call" | custom-call | tf_op jit(solution)/shard_map/attention/pallas_call | solution.py:633
  67.7 48.1 %reduce.1 = (bf16[256,1024]{1,0:T(8,128)(2,1)S(1)}, bf16[256,512]{1,0:T(8,128)(2,1)S(1)}, bf16[256,512]{1,0:T(8,128)(2,1)S(1)}) custom-call(bf16[8,256,1024]{2,1,0:T(8,128)(2,1)S(1)} %bitcast.4, bf16[256,512]{1,0:T(8,128)(2,1)S(1)} %get-tuple-element.16.att_ref, bf16[512,4096]{1,0:T(8,128)(2,1)S(1)} %get-tuple-element.17.w_ref), custom_call_target="tpu_custom_call" | custom-call | tf_op jit(solution)/shard_map/reduce/pallas_call | solution.py:652
  115.8 0.8 copy.14
  116.6 0.7 copy.15
  117.3 0.7 copy.16
Async XLA Ops:
  0.6 53.8 %copy-start.2 = (s32[2]{0:T(128)S(1)}, s32[2]{0:T(128)}, u32[]{:S(2)}) copy-start(s32[2]{0:T(128)} %gb.1) | copy-start | bytes 28
  0.6 53.8 %copy-start.1 = (s32[16,32,3]{1,0,2:T(8,128)S(1)}, s32[16,32,3]{1,0,2:T(8,128)}, u32[]{:S(2)}) copy-start(s32[16,32,3]{1,0,2:T(8,128)} %param.12) | copy-start | bytes 18436
  0.7 53.8 %copy-start = (bf16[256,512]{1,0:T(8,128)(2,1)S(1)}, bf16[256,512]{1,0:T(8,128)(2,1)}, u32[]{:S(2)}) copy-start(bf16[256,512]{1,0:T(8,128)(2,1)} %q_ref.1) | copy-start | bytes 786436
